TPU v7x, 32 devices: a whole 2x2x4 slice. The times are simulated.
32 devices in a mesh: dp: 4 (over x, core), seq: 8 (over z, y).
Axes of the slice: x: 2, y: 2, z: 4, core: 2. Of those that a mesh axis runs over, the one named last changes fastest.
Arguments:
- inputs: bfloat16 [4, 4096, 768], P('dp', 'seq'), may hold values from -6 to 6
- block_mix: bfloat16 [8, 512, 512], P('seq'), may hold values from -0.25 to 0.25
- cross_mix: bfloat16 [512, 8, 8], P('seq'), may hold values from -2 to 2
- cotangent: bfloat16 [4, 4096, 768], P('dp', 'seq'), may hold values from -0.59765625 to 0.59765625
Outputs:
- output: bfloat16 [4, 4096, 768], P('dp', 'seq')
- input_grad: bfloat16 [4, 4096, 768], P('dp', 'seq')
- block_grad: bfloat16 [8, 512, 512], P('seq')
- cross_grad: bfloat16 [512, 8, 8], P('seq')
All inputs are finite; a program needn't handle non-finite values.
Results may differ from a plain program's by a relative error of at most 0.012.
Values may be sent and summed in bfloat16 or wider, within the bound.
A program may use at most 64 MiB of HBM per device.

v0:
```python
import jax
import jax.numpy as jnp
from jax import lax
from jax.sharding import PartitionSpec as P


def local(inputs, block_mix, cross_mix, cotangent):
    h = jnp.einsum("bsr,brc->bsc", block_mix, inputs, preferred_element_type=jnp.float32).astype(
        jnp.bfloat16
    )
    gate = jax.nn.sigmoid(inputs.astype(jnp.float32))
    h_cols = lax.all_to_all(h, "seq", split_axis=1, concat_axis=0, tiled=True)
    z_cols = jnp.einsum(
        "rab,brc->arc", cross_mix, h_cols, preferred_element_type=jnp.float32
    ).astype(jnp.bfloat16)
    z = lax.all_to_all(z_cols, "seq", split_axis=0, concat_axis=1, tiled=True)
    dz = (cotangent.astype(jnp.float32) * gate).astype(jnp.bfloat16)
    dz_cols = lax.all_to_all(dz, "seq", split_axis=1, concat_axis=0, tiled=True)
    dh_cols = jnp.einsum(
        "rab,arc->brc", cross_mix, dz_cols, preferred_element_type=jnp.float32
    ).astype(jnp.bfloat16)
    cross_part = jnp.einsum("arc,brc->rab", dz_cols, h_cols, preferred_element_type=jnp.float32)
    dh = lax.all_to_all(dh_cols, "seq", split_axis=0, concat_axis=1, tiled=True)
    dv = jnp.einsum("bsr,bsc->brc", block_mix, dh, preferred_element_type=jnp.float32)
    block_part = jnp.einsum("bsc,brc->bsr", dh, inputs, preferred_element_type=jnp.float32)
    block_sum, cross_sum = (
        lax.psum(block_part.astype(jnp.bfloat16), "dp").astype(jnp.float32),
        lax.psum(cross_part.astype(jnp.bfloat16), "dp").astype(jnp.float32),
    )
    zf = z.astype(jnp.float32)
    output = (inputs.astype(jnp.float32) + zf * gate).astype(jnp.bfloat16)
    input_grad = (cotangent.astype(jnp.float32) * (1.0 + zf * gate * (1.0 - gate)) + dv).astype(
        jnp.bfloat16
    )
    return (output, input_grad, block_sum.astype(jnp.bfloat16), cross_sum.astype(jnp.bfloat16))


def solution(mesh):
    placed = (
        P("dp", "seq", None),
        P("seq", None, None),
        P("seq", None, None),
        P("dp", "seq", None),
    )
    return jax.shard_map(
        local,
        mesh=mesh,
        in_specs=placed,
        out_specs=(
            P("dp", "seq", None),
            P("dp", "seq", None),
            P("seq", None, None),
            P("seq", None, None),
        ),
        check_vma=False,
    )
```

profile of v0, /device:TPU:0, one launch (start us, length us, event | category | flops | bytes accessed | tf_op | source)
XLA Modules:
  0.0 190.0 jit_solution(17759699037681168629)
XLA Ops:
  7.2 0.0 copy-start
  7.2 1.0 copy-done
  8.2 1.7 fusion.9
  9.9 1.2 copy.73
  11.1 0.5 broadcast.12
  11.7 5.4 %reduce = bf16[512,768]{1,0:T(8,128)(2,1)S(1)} reduce(bf16[512,1,768]{2,1,0:T(2,128)(2,1)S(1)} %bitcast.39, bf16[]{:T(256)} %broadcast.12), dimensions={1}, to_apply=%bitcast.37.reduce_sub_computation | reduce | bytes 1572866
  17.1 0.0 copy-start.8
  17.1 1.1 reshape.57
  18.2 7.3 %all-to-all-start = ((bf16[8,2,24576]{2,1,0:T(2,128)(2,1)}), bf16[8,2,24576]{2,1,0:T(2,128)(2,1)S(1)}, u32[]{:S(2)}, u32[]{:S(2)}) async-start(bf16[8,2,24576]{2,1,0:T(2,128)(2,1)} %reshape.57), calls=%async_computation | async-start | bytes 1572864 | tf_op jit(solution)/shard_map/all_to_all | solution.py:12
  25.4 0.0 copy-done.8
  25.4 0.1 copy.55
  25.6 20.0 %all-to-all-done = bf16[8,2,24576]{2,1,0:T(2,128)(2,1)S(1)} async-done(((bf16[8,2,24576]{2,1,0:T(2,128)(2,1)}), bf16[8,2,24576]{2,1,0:T(2,128)(2,1)S(1)}, u32[]{:S(2)}, u32[]{:S(2)}) %all-to-all-start) | async-done | bytes 786464 | tf_op jit(solution)/shard_map/all_to_all | solution.py:12
  45.6 0.8 reshape.58
  46.4 0.1 copy.62
  46.6 0.0 copy-start.4
  46.6 0.9 copy-done.4
  47.4 0.6 fusion.7
  48.0 1.0 copy.50
  49.1 0.0 copy-start.7
  49.1 3.9 %all-to-all-start.1 = ((bf16[8,64,768]{2,1,0:T(8,128)(2,1)}), bf16[8,64,768]{2,1,0:T(8,128)(2,1)S(1)}, u32[]{:S(2)}, u32[]{:S(2)}) async-start(bf16[8,64,768]{2,1,0:T(8,128)(2,1)} %copy.50), calls=%async_computation.1 | async-start | bytes 1572864 | tf_op jit(solution)/shard_map/all_to_all | solution.py:16
  52.9 1.4 copy.46
  54.3 0.0 copy-done.7
  54.4 1.2 copy.52
  55.5 17.6 %all-to-all-done.1 = bf16[8,64,768]{2,1,0:T(8,128)(2,1)S(1)} async-done(((bf16[8,64,768]{2,1,0:T(8,128)(2,1)}), bf16[8,64,768]{2,1,0:T(8,128)(2,1)S(1)}, u32[]{:S(2)}, u32[]{:S(2)}) %all-to-all-start.1) | async-done | bytes 786464 | tf_op jit(solution)/shard_map/all_to_all | solution.py:16
  73.1 0.0 copy-start.3
  73.1 0.9 copy-done.3
  74.0 1.2 bitcast_convert_fusion
  75.2 1.6 copy.51
  76.8 3.4 %fusion.6 = (bf16[1,512,768]{1,2,0:T(8,128)(2,1)}, bf16[1,512,768]{1,2,0:T(8,128)(2,1)}) fusion(bf16[1,512,768]{1,2,0:T(8,128)(2,1)} %copy.52, bf16[1,512,768]{1,2,0:T(8,128)(2,1)S(1)} %copy.46, f32[1,512,768]{1,2,0:T(8,128)} %copy.51), kind=kLoop, calls=%fused_computation.10 | loop fusion | flops 3932160 | bytes 4718592 | tf_op jit(solution)/shard_map/convert_element_type | solution.py:17
  80.2 3.7 %copy.53 = bf16[1,512,768]{2,0,1:T(2,128)(2,1)S(1)} copy(bf16[1,512,768]{1,2,0:T(8,128)(2,1)} %get-tuple-element.20) | data formatting | bytes 1572864 | tf_op jit(solution)/shard_map/convert_element_type | solution.py:17
  84.0 6.3 %reduce.1 = bf16[512,768]{1,0:T(8,128)(2,1)} reduce(bf16[512,1,768]{2,1,0:T(2,128)(2,1)S(1)} %bitcast.40, bf16[]{:T(256)} %broadcast.12), dimensions={1}, to_apply=%bitcast.30.reduce_sub_computation | reduce | bytes 1572866
  90.3 2.2 %reshape.59 = bf16[8,2,24576]{2,1,0:T(2,128)(2,1)S(1)} reshape(bf16[512,768]{1,0:T(8,128)(2,1)} %reduce.1) | data formatting | bytes 1572864
  92.5 23.8 %all_to_all.42 = bf16[8,2,24576]{2,1,0:T(2,128)(2,1)} all-to-all(bf16[8,2,24576]{2,1,0:T(2,128)(2,1)S(1)} %reshape.59), channel_id=1, replica_groups=mesh['dp'=4,'seq'=8] {'seq'}, dimensions={0} | all-to-all | bytes 1572864 | tf_op jit(solution)/shard_map/all_to_all | solution.py:18
  116.3 4.1 %reshape.60 = bf16[512,1,768]{2,1,0:T(2,128)(2,1)S(1)} reshape(bf16[8,2,24576]{2,1,0:T(2,128)(2,1)} %all_to_all.42) | data formatting | bytes 1572864
  120.4 0.1 copy.63
  120.5 0.0 copy-start.6
  120.5 0.6 fusion.8
  121.1 0.3 copy-done.6
  121.4 0.0 copy-start.2
  121.4 1.0 copy.56
  122.5 0.0 copy-start.5
  122.5 4.3 %all-to-all-start.3 = ((bf16[8,64,768]{2,1,0:T(8,128)(2,1)}), bf16[8,64,768]{2,1,0:T(8,128)(2,1)}, u32[]{:S(2)}, u32[]{:S(2)}) async-start(bf16[8,64,768]{2,1,0:T(8,128)(2,1)} %copy.56), calls=%async_computation.3 | async-start | bytes 1572864 | tf_op jit(solution)/shard_map/all_to_all | solution.py:23
  126.8 0.0 all-reduce.2.cloned.1.call-start
  126.9 0.0 copy-done.2
  126.9 1.2 copy.59
  128.0 0.0 copy-done.5
  128.0 2.1 %convolution_convert_fusion.4 = bf16[64,8,8]{2,1,0:T(8,128)(2,1)S(1)} fusion(bf16[8,64,768]{2,1,0:T(8,128)(2,1)} %bitcast.47, bf16[8,64,768]{2,1,0:T(8,128)(2,1)S(1)} %bitcast.45), kind=kOutput, calls=%fused_computation.19 | convolution fusion | flops 6295552 | bytes 1581056 | tf_op jit(solution)/shard_map/arc,brc->rab/dot_general | solution.py:22
  130.1 12.4 %psum.15 = bf16[64,8,8]{2,1,0:T(8,128)(2,1)S(1)} all-reduce(bf16[64,8,8]{2,1,0:T(8,128)(2,1)S(1)} %convolution_convert_fusion.4), channel_id=1, replica_groups=mesh['dp'=4,'seq'=8] {'dp'}, use_global_device_ids=true, to_apply=%region_1.0 | all-reduce | flops 4096 | bytes 16384 | tf_op jit(solution)/shard_map/psum | solution.py:28
  142.5 0.0 copy-start.1
  142.5 0.7 copy.61
  143.2 3.0 %all-to-all-done.3 = bf16[8,64,768]{2,1,0:T(8,128)(2,1)} async-done(((bf16[8,64,768]{2,1,0:T(8,128)(2,1)}), bf16[8,64,768]{2,1,0:T(8,128)(2,1)}, u32[]{:S(2)}, u32[]{:S(2)}) %all-to-all-start.3) | async-done | bytes 786464 | tf_op jit(solution)/shard_map/all_to_all | solution.py:23
  146.2 2.8 %fusion.10 = bf16[1,512,512]{2,1,0:T(8,128)(2,1)} fusion(bf16[512,768]{1,0:T(8,128)(2,1)} %bitcast.6, bf16[1,512,768]{2,1,0:T(8,128)(2,1)} %param.4), kind=kOutput, calls=%fused_computation.18 | convolution fusion | flops 402915328 | bytes 2097152 | tf_op jit(solution)/shard_map/bsc,brc->bsr/dot_general | solution.py:25
  149.0 0.0 all-reduce.2.cloned.1.call-update
  149.0 0.0 copy-done.1
  149.0 3.2 %fusion.5 = bf16[1,512,768]{1,2,0:T(8,128)(2,1)} fusion(bf16[1,512,768]{1,2,0:T(8,128)(2,1)} %copy.52, bf16[512,768]{1,0:T(8,128)(2,1)} %bitcast.6, f32[1,512,768]{1,2,0:T(8,128)S(1)} %copy-done.1, bf16[1,512,512]{2,1,0:T(8,128)(2,1)S(1)} %copy-done, bf16[1,512,768]{1,2,0:T(8,128)(2,1)S(1)} %copy.46), kind=kOutput, calls=%fused_computation.9 | convolution fusion | flops 407371776 | bytes 5242880 | tf_op jit(solution)/shard_map/bsr,bsc->brc/dot_general | solution.py:24
  152.3 2.3 %copy.60 = bf16[1,512,768]{2,1,0:T(8,128)(2,1)} copy(bf16[1,512,768]{1,2,0:T(8,128)(2,1)} %fusion.5) | data formatting | bytes 1572864
  154.6 26.8 %all-reduce.2.cloned.1.call-done = bf16[1,512,512]{2,1,0:T(8,128)(2,1)} async-done(((bf16[1,512,512]{2,1,0:T(8,128)(2,1)}), bf16[1,512,512]{2,1,0:T(8,128)(2,1)}) %all-reduce.2.cloned.1.call-update) | async-done | bytes 524304 | tf_op jit(solution)/shard_map/psum | solution.py:27
  181.3 1.9 copy.75
Async XLA Ops:
  7.2 1.0 copy-start
  17.1 8.4 %copy-start.8 = (bf16[64,8,8]{0,2,1:T(8,128)(2,1)S(1)}, bf16[64,8,8]{0,2,1:T(8,128)(2,1)}, u32[]{:S(2)}) copy-start(bf16[64,8,8]{0,2,1:T(8,128)(2,1)} %param.6) | copy-start | bytes 24580
  18.2 27.5 %all-to-all-start = ((bf16[8,2,24576]{2,1,0:T(2,128)(2,1)}), bf16[8,2,24576]{2,1,0:T(2,128)(2,1)S(1)}, u32[]{:S(2)}, u32[]{:S(2)}) async-start(bf16[8,2,24576]{2,1,0:T(2,128)(2,1)} %reshape.57), calls=%async_computation | async-start | bytes 1572864 | tf_op jit(solution)/shard_map/all_to_all | solution.py:12
  46.6 0.9 copy-start.4
  49.1 5.3 %copy-start.7 = (bf16[1,512,768]{2,1,0:T(8,128)(2,1)S(1)}, bf16[1,512,768]{2,1,0:T(8,128)(2,1)}, u32[]{:S(2)}) copy-start(bf16[1,512,768]{2,1,0:T(8,128)(2,1)} %param.7) | copy-start | bytes 2359300
  49.1 24.0 %all-to-all-start.1 = ((bf16[8,64,768]{2,1,0:T(8,128)(2,1)}), bf16[8,64,768]{2,1,0:T(8,128)(2,1)S(1)}, u32[]{:S(2)}, u32[]{:S(2)}) async-start(bf16[8,64,768]{2,1,0:T(8,128)(2,1)} %copy.50), calls=%async_computation.1 | async-start | bytes 1572864 | tf_op jit(solution)/shard_map/all_to_all | solution.py:16
  73.1 0.9 copy-start.3
  120.5 0.9 copy-start.6
  121.4 5.4 %copy-start.2 = (bf16[1,512,768]{1,2,0:T(8,128)(2,1)S(1)}, bf16[1,512,768]{1,2,0:T(8,128)(2,1)}, u32[]{:S(2)}) copy-start(bf16[1,512,768]{1,2,0:T(8,128)(2,1)} %get-tuple-element.21) | copy-start | bytes 2359300
  122.5 5.6 %copy-start.5 = (bf16[1,512,768]{2,1,0:T(8,128)(2,1)S(1)}, bf16[1,512,768]{2,1,0:T(8,128)(2,1)}, u32[]{:S(2)}) copy-start(bf16[1,512,768]{2,1,0:T(8,128)(2,1)} %copy-done.4) | copy-start | bytes 2359300
  122.5 23.8 %all-to-all-start.3 = ((bf16[8,64,768]{2,1,0:T(8,128)(2,1)}), bf16[8,64,768]{2,1,0:T(8,128)(2,1)}, u32[]{:S(2)}, u32[]{:S(2)}) async-start(bf16[8,64,768]{2,1,0:T(8,128)(2,1)} %copy.56), calls=%async_computation.3 | async-start | bytes 1572864 | tf_op jit(solution)/shard_map/all_to_all | solution.py:23
  126.8 54.5 %all-reduce.2.cloned.1.call-start = ((), (), s32[]{:S(2)}) async-start(), calls=%async_computation.4 | async-start | bytes 1048576 | tf_op jit(solution)/shard_map/psum | solution.py:27
  142.5 6.5 %copy-start.1 = (f32[1,512,768]{1,2,0:T(8,128)S(1)}, f32[1,512,768]{1,2,0:T(8,128)}, u32[]{:S(2)}) copy-start(f32[1,512,768]{1,2,0:T(8,128)} %copy.51) | copy-start | bytes 4718596
Sparse Core Ops, SparseCore 0:
  149.2 32.1 all-reduce.1
where the time goes:
time: 191 us; the launch traced here: 190 us
  waiting for transfers between devices  67.4 us (35%)
  blocking collectives  36.1 us (19%)
  local copies, waits for them, and re-layouts  29.5 us (15%)
  other arithmetic  16.4 us (9%)
  starting transfers between devices  15.5 us (8%)
  between operations  14.2 us (7%)
  matrix products  10.9 us (6%)
    psum x1, waiting for transfers between devices, local(): lax.psum(block_part.astype(jnp.bfloat16), 'dp').astype(jnp.float32)  26.8 us
    all_to_all x1, blocking collectives, local(): dz_cols = lax.all_to_all(dz, 'seq', split_axis=1, concat_axis=0, tiled=True)  23.8 us
    unnamed x32, local copies, waits for them, and re-layouts  20.9 us
    all_to_all x1, waiting for transfers between devices, local(): h_cols = lax.all_to_all(h, 'seq', split_axis=1, concat_axis=0, tiled=True)  20 us
    all_to_all x1, waiting for transfers between devices, local(): z = lax.all_to_all(z_cols, 'seq', split_axis=0, concat_axis=1, tiled=True)  17.6 us
    psum x1, blocking collectives, local(): lax.psum(cross_part.astype(jnp.bfloat16), 'dp').astype(jnp.float32)  12.4 us
    unnamed x2, other arithmetic  11.7 us
    all_to_all x1, starting transfers between devices, local(): h_cols = lax.all_to_all(h, 'seq', split_axis=1, concat_axis=0, tiled=True)  7.28 us
  transfers between devices with their start and end apart: 4, of which 4 were waited for; matrix products, arithmetic and copies ran while one was open for 6% of the time, Pallas kernels for 0%

commit v1 on v0

--- a/solution.py
+++ b/solution.py
@@ -2,6 +2,18 @@
 import jax.numpy as jnp
 from jax import lax
 from jax.sharding import PartitionSpec as P
+
+
+def sent_to_each(shard, axis, split, join):
+    ways, here = (lax.axis_size(axis), lax.axis_index(axis))
+    width = shard.shape[split] // ways
+    turned = jnp.roll(shard, -here * width, axis=split)
+    got = [lax.slice_in_dim(turned, 0, width, axis=split)]
+    for far in range(1, ways):
+        sent = lax.slice_in_dim(turned, far * width, (far + 1) * width, axis=split)
+        got.append(lax.ppermute(sent, axis, [(d, (d + far) % ways) for d in range(ways)]))
+    line = jnp.concatenate(got[::-1], axis=join)
+    return jnp.roll(line, (here + 1) * got[0].shape[join], axis=join)
 
 
 def local(inputs, block_mix, cross_mix, cotangent):
@@ -13,7 +25,7 @@
     z_cols = jnp.einsum(
         "rab,brc->arc", cross_mix, h_cols, preferred_element_type=jnp.float32
     ).astype(jnp.bfloat16)
-    z = lax.all_to_all(z_cols, "seq", split_axis=0, concat_axis=1, tiled=True)
+    z = sent_to_each(z_cols, "seq", 0, 1)
     dz = (cotangent.astype(jnp.float32) * gate).astype(jnp.bfloat16)
     dz_cols = lax.all_to_all(dz, "seq", split_axis=1, concat_axis=0, tiled=True)
     dh_cols = jnp.einsum(

time: 191 us -> 178 us (0.932)
  local copies, waits for them, and re-layouts: 29.5 us -> 12.7 us
  starting transfers between devices: 15.5 us -> 29.3 us
  waiting for transfers between devices: 67.4 us -> 62.7 us
  other arithmetic: 16.4 us -> 12.7 us
    ppermute x0 -> x7, starting transfers between devices: none -> 18.4 us  [sent_to_each(): lax.ppermute(sent, axis, [(d, (d + far) % ways) for d in range(ways)])]
    all_to_all x1 -> x0, waiting for transfers between devices: 17.6 us -> none  [local(): z = lax.all_to_all(z_cols, 'seq', split_axis=0, concat_axis=1, tiled=True)]
    unnamed x32 -> x43, local copies, waits for them, and re-layouts: 20.9 us -> 8.4 us
    ppermute x0 -> x7, waiting for transfers between devices: none -> 7.42 us  [sent_to_each(): lax.ppermute(sent, axis, [(d, (d + far) % ways) for d in range(ways)])]
    all_to_all x1 -> x0, starting transfers between devices: 3.86 us -> none  [local(): z = lax.all_to_all(z_cols, 'seq', split_axis=0, concat_axis=1, tiled=True)]
    all_to_all x1, waiting for transfers between devices: 3.01 us -> 6.09 us  [local(): dh = lax.all_to_all(dh_cols, 'seq', split_axis=0, concat_axis=1, tiled=True)]
    convert_element_type x2 -> x0, local copies, waits for them, and re-layouts: 2.63 us -> none  [the longest x1 1.62 us: local(): zf = z.astype(jnp.float32)]
    convert_element_type x1, local copies, waits for them, and re-layouts: 3.72 us -> 1.21 us  [local(): dz = (cotangent.astype(jnp.float32) * gate).astype(jnp.bfloat16)]
  transfers between devices with their start and end apart: 4 -> 10, of which waited for: 4 -> 5; matrix products, arithmetic and copies ran while one was open for 6% -> 3% of each run, Pallas kernels for 0% -> 0%
where the time goes in v1:
time: 178 us; the launch traced here: 177 us
  waiting for transfers between devices  62.7 us (35%)
  blocking collectives  36 us (20%)
  starting transfers between devices  29.3 us (16%)
  between operations  14.4 us (8%)
  local copies, waits for them, and re-layouts  12.7 us (7%)
  other arithmetic  12.7 us (7%)
  matrix products  9.37 us (5%)
    psum x1, waiting for transfers between devices, local(): lax.psum(block_part.astype(jnp.bfloat16), 'dp').astype(jnp.float32)  29.2 us
    all_to_all x1, blocking collectives, local(): dz_cols = lax.all_to_all(dz, 'seq', split_axis=1, concat_axis=0, tiled=True)  24.1 us
    all_to_all x1, waiting for transfers between devices, local(): h_cols = lax.all_to_all(h, 'seq', split_axis=1, concat_axis=0, tiled=True)  20 us
    ppermute x7, starting transfers between devices, sent_to_each(): lax.ppermute(sent, axis, [(d, (d + far) % ways) for d in range(ways)])  18.4 us
    psum x1, blocking collectives, local(): lax.psum(cross_part.astype(jnp.bfloat16), 'dp').astype(jnp.float32)  11.9 us
    unnamed x2, other arithmetic  10.9 us
    unnamed x43, local copies, waits for them, and re-layouts  8.4 us
    ppermute x7, waiting for transfers between devices, sent_to_each(): lax.ppermute(sent, axis, [(d, (d + far) % ways) for d in range(ways)])  7.42 us
  transfers between devices with their start and end apart: 10, of which 5 were waited for; matrix products, arithmetic and copies ran while one was open for 3% of the time, Pallas kernels for 0%

profile of v1, /device:TPU:0, one launch (start us, length us, event | category | flops | bytes accessed | tf_op | source)
XLA Modules:
  0.0 177.2 jit_solution(1749609339046484815)
XLA Ops:
  7.2 0.0 copy-start
  7.2 1.0 copy-done
  8.2 1.7 fusion.8
  9.9 1.2 copy.100
  11.1 0.5 broadcast.14
  11.7 5.4 %reduce = bf16[512,768]{1,0:T(8,128)(2,1)S(1)} reduce(bf16[512,1,768]{2,1,0:T(2,128)(2,1)S(1)} %bitcast.38, bf16[]{:T(256)} %broadcast.14), dimensions={1}, to_apply=%bitcast.37.reduce_sub_computation | reduce | bytes 1572866
  17.1 0.0 copy-start.8
  17.1 1.1 reshape.39
  18.2 7.3 %all-to-all-start = ((bf16[8,2,24576]{2,1,0:T(2,128)(2,1)}), bf16[8,2,24576]{2,1,0:T(2,128)(2,1)S(1)}, u32[]{:S(2)}, u32[]{:S(2)}) async-start(bf16[8,2,24576]{2,1,0:T(2,128)(2,1)} %reshape.39), calls=%async_computation | async-start | bytes 1572864 | tf_op jit(solution)/shard_map/all_to_all | solution.py:24
  25.4 0.0 copy-done.8
  25.4 0.1 copy.76
  25.6 20.0 %all-to-all-done = bf16[8,2,24576]{2,1,0:T(2,128)(2,1)S(1)} async-done(((bf16[8,2,24576]{2,1,0:T(2,128)(2,1)}), bf16[8,2,24576]{2,1,0:T(2,128)(2,1)S(1)}, u32[]{:S(2)}, u32[]{:S(2)}) %all-to-all-start) | async-done | bytes 786464 | tf_op jit(solution)/shard_map/all_to_all | solution.py:24
  45.6 0.8 reshape.40
  46.4 0.1 copy.83
  46.6 0.0 copy-start.1
  46.6 0.9 copy-done.1
  47.4 0.6 fusion.17
  48.0 0.1 copy.98
  48.2 0.3 fusion.11
  48.5 0.7 fusion.21
  49.2 2.3 %collective-permute-start = (bf16[1,64,768]{2,1,0:T(8,128)(2,1)S(1)}, bf16[1,64,768]{2,1,0:T(8,128)(2,1)S(1)}, u32[]{:S(2)}, u32[]{:S(2)}) collective-permute-start(bf16[1,64,768]{2,1,0:T(8,128)(2,1)S(1)} %get-tuple-element.36), channel_id=1, source_target_pairs={{0,7},{1,0},{2,1},{3,2},{4,3},{5,4},{6,5},{7,6},{8,15},{9,8},{10,9... | collective-permute-start | bytes 294920 | tf_op jit(solution)/shard_map/ppermute | solution.py:14
  51.5 0.0 collective-permute-start.6
  51.5 0.6 collective-permute-start.5
  52.1 1.1 collective-permute-start.4
  53.2 4.2 %collective-permute-start.3 = (bf16[1,64,768]{2,1,0:T(8,128)(2,1)S(1)}, bf16[1,64,768]{2,1,0:T(8,128)(2,1)S(1)}, u32[]{:S(2)}, u32[]{:S(2)}) collective-permute-start(bf16[1,64,768]{2,1,0:T(8,128)(2,1)S(1)} %get-tuple-element.33), channel_id=1, source_target_pairs={{0,4},{1,5},{2,6},{3,7},{4,0},{5,1},{6,2},{7,3},{8,12},{9,13},{10,... | collective-permute-start | bytes 294920 | tf_op jit(solution)/shard_map/ppermute | solution.py:14
  57.3 0.0 collective-permute-done
  57.3 2.4 %collective-permute-start.1 = (bf16[1,64,768]{2,1,0:T(8,128)(2,1)}, bf16[1,64,768]{2,1,0:T(8,128)(2,1)S(1)}, u32[]{:S(2)}, u32[]{:S(2)}) collective-permute-start(bf16[1,64,768]{2,1,0:T(8,128)(2,1)} %get-tuple-element.35), channel_id=1, source_target_pairs={{0,6},{1,7},{2,0},{3,1},{4,2},{5,3},{6,4},{7,5},{8,14},{9,15},{10,... | collective-permute-start | bytes 294920 | tf_op jit(solution)/shard_map/ppermute | solution.py:14
  59.7 3.3 %collective-permute-done.1 = bf16[1,64,768]{2,1,0:T(8,128)(2,1)S(1)} collective-permute-done((bf16[1,64,768]{2,1,0:T(8,128)(2,1)}, bf16[1,64,768]{2,1,0:T(8,128)(2,1)S(1)}, u32[]{:S(2)}, u32[]{:S(2)}) %collective-permute-start.1) | collective-permute-done | bytes 98336 | tf_op jit(solution)/shard_map/ppermute | solution.py:14
  63.0 7.9 %collective-permute-start.2 = (bf16[1,64,768]{2,1,0:T(8,128)(2,1)}, bf16[1,64,768]{2,1,0:T(8,128)(2,1)S(1)}, u32[]{:S(2)}, u32[]{:S(2)}) collective-permute-start(bf16[1,64,768]{2,1,0:T(8,128)(2,1)} %get-tuple-element.34), channel_id=1, source_target_pairs={{0,5},{1,6},{2,7},{3,0},{4,1},{5,2},{6,3},{7,4},{8,13},{9,14},{10,... | collective-permute-start | bytes 294920 | tf_op jit(solution)/shard_map/ppermute | solution.py:14
  70.9 4.1 %collective-permute-done.2 = bf16[1,64,768]{2,1,0:T(8,128)(2,1)S(1)} collective-permute-done((bf16[1,64,768]{2,1,0:T(8,128)(2,1)}, bf16[1,64,768]{2,1,0:T(8,128)(2,1)S(1)}, u32[]{:S(2)}, u32[]{:S(2)}) %collective-permute-start.2) | collective-permute-done | bytes 98336 | tf_op jit(solution)/shard_map/ppermute | solution.py:14
  75.0 0.0 collective-permute-done.3
  75.0 0.0 collective-permute-done.4
  75.1 0.0 collective-permute-done.5
  75.1 0.0 collective-permute-done.6
  75.3 0.0 copy-done.3
  75.3 0.0 copy-done.5
  75.3 0.0 copy-start.7
  75.3 1.5 fusion.6
  76.8 0.0 copy-done.7
  76.8 1.2 copy.99
  78.1 5.4 %reduce.1 = bf16[512,768]{1,0:T(8,128)(2,1)S(1)} reduce(bf16[512,1,768]{2,1,0:T(2,128)(2,1)S(1)} %bitcast.39, bf16[]{:T(256)} %broadcast.14), dimensions={1}, to_apply=%bitcast.36.reduce_sub_computation | reduce | bytes 1572866
  83.5 0.2 reshape.41
  83.7 24.1 %all_to_all.33 = bf16[8,2,24576]{2,1,0:T(2,128)(2,1)S(1)} all-to-all(bf16[8,2,24576]{2,1,0:T(2,128)(2,1)S(1)} %reshape.41), channel_id=1, replica_groups=mesh['dp'=4,'seq'=8] {'seq'}, dimensions={0} | all-to-all | bytes 1572864 | tf_op jit(solution)/shard_map/all_to_all | solution.py:30
  107.8 0.8 reshape.42
  108.6 0.1 copy.84
  108.7 0.6 fusion.7
  109.3 0.0 copy-start.2
  109.3 1.0 copy.77
  110.3 3.6 %all-to-all-start.2 = ((bf16[8,64,768]{2,1,0:T(8,128)(2,1)}), bf16[8,64,768]{2,1,0:T(8,128)(2,1)S(1)}, u32[]{:S(2)}, u32[]{:S(2)}) async-start(bf16[8,64,768]{2,1,0:T(8,128)(2,1)} %copy.77), calls=%async_computation.2 | async-start | bytes 1572864 | tf_op jit(solution)/shard_map/all_to_all | solution.py:35
  113.9 0.0 all-reduce.2.cloned.1.call-start
  113.9 0.0 copy-done.2
  114.0 0.9 convolution_convert_fusion.3
  114.9 11.9 %psum.15 = bf16[64,8,8]{2,1,0:T(8,128)(2,1)S(1)} all-reduce(bf16[64,8,8]{2,1,0:T(8,128)(2,1)S(1)} %convolution_convert_fusion.3), channel_id=1, replica_groups=mesh['dp'=4,'seq'=8] {'dp'}, use_global_device_ids=true, to_apply=%region_1.2 | all-reduce | flops 4096 | bytes 16384 | tf_op jit(solution)/shard_map/psum | solution.py:40
  126.8 0.0 copy-start.4
  126.8 0.0 copy-start.6
  126.8 0.7 copy.81
  127.6 6.1 %all-to-all-done.2 = bf16[8,64,768]{2,1,0:T(8,128)(2,1)S(1)} async-done(((bf16[8,64,768]{2,1,0:T(8,128)(2,1)}), bf16[8,64,768]{2,1,0:T(8,128)(2,1)S(1)}, u32[]{:S(2)}, u32[]{:S(2)}) %all-to-all-start.2) | async-done | bytes 786464 | tf_op jit(solution)/shard_map/all_to_all | solution.py:35
  133.7 2.5 %fusion.9 = bf16[1,512,512]{2,1,0:T(8,128)(2,1)} fusion(bf16[512,768]{1,0:T(8,128)(2,1)S(1)} %bitcast.47, bf16[1,512,768]{2,1,0:T(8,128)(2,1)} %param.4), kind=kOutput, calls=%fused_computation.20 | convolution fusion | flops 402915328 | bytes 2097152 | tf_op jit(solution)/shard_map/bsc,brc->bsr/dot_general | solution.py:37
  136.2 0.0 all-reduce.2.cloned.1.call-update
  136.2 0.0 copy-done.4
  136.2 0.0 copy-done.6
  136.2 3.0 %fusion.5 = bf16[1,512,768]{2,1,0:T(8,128)(2,1)} fusion(bf16[1,512,768]{2,1,0:T(8,128)(2,1)S(1)} %copy-done.4, bf16[512,768]{1,0:T(8,128)(2,1)S(1)} %bitcast.48, bf16[1,1024,768]{2,1,0:T(8,128)(2,1)} %copy-done.7, s32[]{:T(128)S(6)} %select_n.26, bf16[1,512,512]{2,1,0:T(8,128)(2,1)S(1)} %copy-done, bf16[1,512,768]{2,1,0:T(8,128)(2,1)S(1)} %copy-done.6), kind=kOutput, calls=%fused_computation.9 | convolution fusion | flops 407764992 | bytes 4456452 | tf_op jit(solution)/shard_map/bsr,bsc->brc/dot_general | solution.py:36
  139.3 29.2 %all-reduce.2.cloned.1.call-done = bf16[1,512,512]{2,1,0:T(8,128)(2,1)} async-done(((bf16[1,512,512]{2,1,0:T(8,128)(2,1)}), bf16[1,512,512]{2,1,0:T(8,128)(2,1)}) %all-reduce.2.cloned.1.call-update) | async-done | bytes 524304 | tf_op jit(solution)/shard_map/psum | solution.py:39
  168.4 1.9 %copy.117 = bf16[1,512,512]{2,1,0:T(8,128)(2,1)} copy(bf16[1,512,512]{2,1,0:T(8,128)(2,1)} %all-reduce.2.cloned.1.call-done) | data formatting | bytes 1048576
  (18 shorter events, 0.1 us)
Async XLA Ops:
  7.2 1.0 copy-start
  17.1 8.4 %copy-start.8 = (bf16[64,8,8]{0,2,1:T(8,128)(2,1)S(1)}, bf16[64,8,8]{0,2,1:T(8,128)(2,1)}, u32[]{:S(2)}) copy-start(bf16[64,8,8]{0,2,1:T(8,128)(2,1)} %param.6) | copy-start | bytes 24580
  18.2 27.5 %all-to-all-start = ((bf16[8,2,24576]{2,1,0:T(2,128)(2,1)}), bf16[8,2,24576]{2,1,0:T(2,128)(2,1)S(1)}, u32[]{:S(2)}, u32[]{:S(2)}) async-start(bf16[8,2,24576]{2,1,0:T(2,128)(2,1)} %reshape.39), calls=%async_computation | async-start | bytes 1572864 | tf_op jit(solution)/shard_map/all_to_all | solution.py:24
  46.6 0.9 copy-start.1
  49.2 8.1 %collective-permute-start = (bf16[1,64,768]{2,1,0:T(8,128)(2,1)S(1)}, bf16[1,64,768]{2,1,0:T(8,128)(2,1)S(1)}, u32[]{:S(2)}, u32[]{:S(2)}) collective-permute-start(bf16[1,64,768]{2,1,0:T(8,128)(2,1)S(1)} %get-tuple-element.36), channel_id=1, source_target_pairs={{0,7},{1,0},{2,1},{3,2},{4,3},{5,4},{6,5},{7,6},{8,15},{9,8},{10,9... | collective-permute-start | bytes 294920 | tf_op jit(solution)/shard_map/ppermute | solution.py:14
  51.5 23.6 %collective-permute-start.6 = (bf16[1,64,768]{2,1,0:T(8,128)(2,1)S(1)}, bf16[1,64,768]{2,1,0:T(8,128)(2,1)S(1)}, u32[]{:S(2)}, u32[]{:S(2)}) collective-permute-start(bf16[1,64,768]{2,1,0:T(8,128)(2,1)S(1)} %get-tuple-element.30), channel_id=1, source_target_pairs={{0,1},{1,2},{2,3},{3,4},{4,5},{5,6},{6,7},{7,0},{8,9},{9,10},{10,1... | collective-permute-start | bytes 294920 | tf_op jit(solution)/shard_map/ppermute | solution.py:14
  51.5 23.6 %collective-permute-start.5 = (bf16[1,64,768]{2,1,0:T(8,128)(2,1)S(1)}, bf16[1,64,768]{2,1,0:T(8,128)(2,1)S(1)}, u32[]{:S(2)}, u32[]{:S(2)}) collective-permute-start(bf16[1,64,768]{2,1,0:T(8,128)(2,1)S(1)} %get-tuple-element.31), channel_id=1, source_target_pairs={{0,2},{1,3},{2,4},{3,5},{4,6},{5,7},{6,0},{7,1},{8,10},{9,11},{10,... | collective-permute-start | bytes 294920 | tf_op jit(solution)/shard_map/ppermute | solution.py:14
  52.1 23.0 %collective-permute-start.4 = (bf16[1,64,768]{2,1,0:T(8,128)(2,1)S(1)}, bf16[1,64,768]{2,1,0:T(8,128)(2,1)S(1)}, u32[]{:S(2)}, u32[]{:S(2)}) collective-permute-start(bf16[1,64,768]{2,1,0:T(8,128)(2,1)S(1)} %get-tuple-element.32), channel_id=1, source_target_pairs={{0,3},{1,4},{2,5},{3,6},{4,7},{5,0},{6,1},{7,2},{8,11},{9,12},{10,... | collective-permute-start | bytes 294920 | tf_op jit(solution)/shard_map/ppermute | solution.py:14
  53.2 21.9 %collective-permute-start.3 = (bf16[1,64,768]{2,1,0:T(8,128)(2,1)S(1)}, bf16[1,64,768]{2,1,0:T(8,128)(2,1)S(1)}, u32[]{:S(2)}, u32[]{:S(2)}) collective-permute-start(bf16[1,64,768]{2,1,0:T(8,128)(2,1)S(1)} %get-tuple-element.33), channel_id=1, source_target_pairs={{0,4},{1,5},{2,6},{3,7},{4,0},{5,1},{6,2},{7,3},{8,12},{9,13},{10,... | collective-permute-start | bytes 294920 | tf_op jit(solution)/shard_map/ppermute | solution.py:14
  57.3 17.9 %copy-start.3 = (bf16[1,512,768]{2,1,0:T(8,128)(2,1)S(1)}, bf16[1,512,768]{2,1,0:T(8,128)(2,1)}, u32[]{:S(2)}) copy-start(bf16[1,512,768]{2,1,0:T(8,128)(2,1)} %param.7) | copy-start | bytes 2359300
  57.3 17.9 %copy-start.5 = (bf16[1,512,768]{2,1,0:T(8,128)(2,1)S(1)}, bf16[1,512,768]{2,1,0:T(8,128)(2,1)}, u32[]{:S(2)}) copy-start(bf16[1,512,768]{2,1,0:T(8,128)(2,1)} %param.4) | copy-start | bytes 2359300
  57.3 5.7 %collective-permute-start.1 = (bf16[1,64,768]{2,1,0:T(8,128)(2,1)}, bf16[1,64,768]{2,1,0:T(8,128)(2,1)S(1)}, u32[]{:S(2)}, u32[]{:S(2)}) collective-permute-start(bf16[1,64,768]{2,1,0:T(8,128)(2,1)} %get-tuple-element.35), channel_id=1, source_target_pairs={{0,6},{1,7},{2,0},{3,1},{4,2},{5,3},{6,4},{7,5},{8,14},{9,15},{10,... | collective-permute-start | bytes 294920 | tf_op jit(solution)/shard_map/ppermute | solution.py:14
  63.0 12.0 %collective-permute-start.2 = (bf16[1,64,768]{2,1,0:T(8,128)(2,1)}, bf16[1,64,768]{2,1,0:T(8,128)(2,1)S(1)}, u32[]{:S(2)}, u32[]{:S(2)}) collective-permute-start(bf16[1,64,768]{2,1,0:T(8,128)(2,1)} %get-tuple-element.34), channel_id=1, source_target_pairs={{0,5},{1,6},{2,7},{3,0},{4,1},{5,2},{6,3},{7,4},{8,13},{9,14},{10,... | collective-permute-start | bytes 294920 | tf_op jit(solution)/shard_map/ppermute | solution.py:14
  75.3 1.5 copy-start.7
  109.3 4.7 %copy-start.2 = (bf16[1,512,768]{2,1,0:T(8,128)(2,1)S(1)}, bf16[1,512,768]{2,1,0:T(8,128)(2,1)}, u32[]{:S(2)}) copy-start(bf16[1,512,768]{2,1,0:T(8,128)(2,1)} %copy-done.1) | copy-start | bytes 2359300
  110.3 23.3 %all-to-all-start.2 = ((bf16[8,64,768]{2,1,0:T(8,128)(2,1)}), bf16[8,64,768]{2,1,0:T(8,128)(2,1)S(1)}, u32[]{:S(2)}, u32[]{:S(2)}) async-start(bf16[8,64,768]{2,1,0:T(8,128)(2,1)} %copy.77), calls=%async_computation.2 | async-start | bytes 1572864 | tf_op jit(solution)/shard_map/all_to_all | solution.py:35
  113.9 54.5 %all-reduce.2.cloned.1.call-start = ((), (), s32[]{:S(2)}) async-start(), calls=%async_computation.3 | async-start | bytes 1048576 | tf_op jit(solution)/shard_map/psum | solution.py:39
  126.8 9.4 %copy-start.4 = (bf16[1,512,768]{2,1,0:T(8,128)(2,1)S(1)}, bf16[1,512,768]{2,1,0:T(8,128)(2,1)}, u32[]{:S(2)}) copy-start(bf16[1,512,768]{2,1,0:T(8,128)(2,1)} %param.7) | copy-start | bytes 2359300
  126.8 9.4 %copy-start.6 = (bf16[1,512,768]{2,1,0:T(8,128)(2,1)S(1)}, bf16[1,512,768]{2,1,0:T(8,128)(2,1)}, u32[]{:S(2)}) copy-start(bf16[1,512,768]{2,1,0:T(8,128)(2,1)} %param.4) | copy-start | bytes 2359300
Sparse Core Ops, SparseCore 0:
  136.3 32.0 all-reduce.1
